TPU v7x, 256 devices: a whole 4x4x8 slice. The times are simulated.
256 devices in a mesh: pair: 32 (over x, y, core), virt: 8 (over z).
Axes of the slice: x: 4, y: 4, z: 8, core: 2. Of those that a mesh axis runs over, the one named last changes fastest.
Arguments:
- amps: float32 [8, 2048, 2048], P(None, 'pair', 'virt'), may hold values from -6 to 6
- ints: float32 [8, 2048, 2048], P(None, 'pair', 'virt'), may hold values from -0.125 to 0.125
- panel_of: int32 [32], replicated, may hold values from 0 to 31, each once
- e_occ: float32 [8], replicated, may hold values from -2 to -0.5
- e_vir: float32 [2048], replicated, may hold values from 0.2 to 3
Outputs:
- cycle_update: float32 [8, 8, 2048, 2048], P('virt', None, 'pair')
Inputs may be any that keep to these rules, and one draw needn't show every extreme that they name: panel_of holds each of 0 to 31 once.
All inputs are finite; a program needn't handle non-finite values.
Results may differ from a plain program's by a relative error of at most 0.00007.
Values sent between devices are 32-bit elements; how exact they have to be, the bound alone decides.
No kernel may reach another device: no remote copies, remote signals or barrier semaphores. Data moves between devices by JAX's collectives and lax.ppermute only.
A program may use at most 192 MiB of HBM per device.

v0:
```python
import jax
import jax.numpy as jnp
from jax import lax
from jax.sharding import PartitionSpec as P


def panel_table(panel_of):
    count = panel_of.shape[0]
    targets = jnp.arange(count, dtype=jnp.int32)
    return (panel_of[:, None] == targets[None, :]).astype(jnp.float32)


def body(amps, ints, panel_of, e_occ, e_vir):
    panel = amps.shape[1]
    occ_all = amps.shape[0]
    n_virt = lax.axis_size("virt")
    n_pair = lax.axis_size("pair")
    occ_dev = occ_all // n_virt
    virtuals = e_vir.shape[0]
    placing = panel_table(panel_of)
    my_occ = lax.axis_index("virt") * occ_dev + jnp.arange(occ_dev, dtype=jnp.int32)
    b_rows = lax.axis_index("pair") * panel + jnp.arange(panel, dtype=jnp.int32)
    e_b = e_vir[b_rows]
    denom = (
        e_occ[my_occ][:, None, None, None]
        + e_occ[None, :, None, None]
        - e_b[None, None, :, None]
        - e_vir[None, None, None, :]
    )
    own_rows = lax.all_to_all(amps, "virt", split_axis=0, concat_axis=2, tiled=True)
    int_full = lax.all_gather(ints, "virt", axis=2, tiled=True)
    product = jnp.einsum(
        "xac,jbc->xjba",
        lax.all_gather(own_rows, "pair", axis=1, tiled=True),
        int_full,
        precision=lax.Precision.HIGHEST,
        preferred_element_type=jnp.float32,
    )
    grouped = product.reshape(occ_dev, occ_all, panel, n_pair, panel)
    direct = jnp.einsum(
        "xjbqp,qn->xjbnp",
        grouped,
        placing,
        precision=lax.Precision.HIGHEST,
        preferred_element_type=jnp.float32,
    ).reshape(occ_dev, occ_all, panel, virtuals)
    mirrored = lax.all_to_all(direct, "virt", split_axis=1, concat_axis=1, tiled=True)
    return (direct - mirrored) / denom


def solution(mesh):
    in_specs = (P(None, "pair", "virt"), P(None, "pair", "virt"), P(), P(), P())
    out_specs = P("virt", None, "pair", None)
    return jax.shard_map(body, mesh=mesh, in_specs=in_specs, out_specs=out_specs, check_vma=False)
```

profile of v0, /device:TPU:1, one launch (start us, length us, event | category | flops | bytes accessed | tf_op | source)
XLA Modules:
  0.0 342.6 jit_solution(10947563948808677150)
XLA Ops:
  6.5 0.0 all-gather.3.cloned.1.call-start
  6.5 0.7 all-gather.3.cloned.1.call-update
  7.3 0.0 all-gather.5.cloned.1.call-start
  7.3 26.2 %all_to_all.23 = f32[8,64,256]{2,1,0:T(8,128)S(1)} all-to-all(f32[8,64,256]{2,1,0:T(8,128)} %param.5), channel_id=1, replica_groups=mesh['pair'=32,'virt'=8] {'virt'}, dimensions={0} | all-to-all | bytes 1048576 | tf_op jit(solution)/shard_map/all_to_all | solution.py:30
  33.5 0.8 copy.14
  34.3 0.0 all-gather.5.cloned.1.call-update
  34.4 37.2 %all-gather.3.cloned.1.call-done = f32[8,64,2048]{2,1,0:T(8,128)} async-done(((f32[8,64,256]{2,1,0:T(8,128)}), f32[8,64,2048]{2,1,0:T(8,128)}) %all-gather.3.cloned.1.call-update) | async-done | bytes 4194320 | tf_op jit(solution)/shard_map/all_gather | solution.py:31
  71.6 79.3 %all-gather.5.cloned.1.call-done = f32[1,2048,2048]{2,1,0:T(8,128)} async-done(((f32[1,64,2048]{2,1,0:T(8,128)}), f32[1,2048,2048]{2,1,0:T(8,128)}) %all-gather.5.cloned.1.call-update) | async-done | bytes 16777232 | tf_op jit(solution)/shard_map/all_gather | solution.py:34
  150.9 0.0 copy-start.1
  150.9 57.1 %fusion.2 = f32[8,64,32,64]{3,1,2,0:T(8,128)S(1)} fusion(f32[32,64,2048,1]{2,1,0,3:T(8,128)} %bitcast.38, f32[8,64,2048]{2,1,0:T(8,128)} %all-gather.3.cloned.1.call-done), kind=kOutput, calls=%fused_computation.3 | convolution fusion | flops 25769803776 | bytes 25165824 | tf_op jit(solution)/shard_map/xac,jbc->xjba/dot_general | solution.py:32
  208.0 0.0 copy-done.1
  208.0 10.1 %fusion.4 = f32[1,8,64,32,64]{4,3,2,1,0:T(8,128)} fusion(f32[8,64,32,64]{3,1,2,0:T(8,128)S(1)} %fusion.2, s32[32]{0:T(128)S(1)} %copy-done.1), kind=kOutput, calls=%fused_computation.6 | convolution fusion | flops 402654208 | bytes 8388736 | tf_op jit(solution)/shard_map/xjbqp,qn->xjbnp/dot_general | solution.py:40
  218.1 7.8 %reshape.79 = f32[1,8,64,2048]{3,2,1,0:T(8,128)} reshape(f32[1,8,64,32,64]{4,3,2,1,0:T(8,128)} %fusion.4) | data formatting | bytes 8388608 | tf_op jit(solution)/shard_map/reshape | solution.py:46
  225.9 0.0 copy-start
  225.9 0.0 copy-start.2
  225.9 6.9 %all-to-all-start.1 = ((f32[1,8,64,2048]{3,2,0,1:T(8,128)}), f32[1,8,64,2048]{3,2,0,1:T(8,128)}, u32[]{:S(2)}, u32[]{:S(2)}) async-start(f32[1,8,64,2048]{3,2,0,1:T(8,128)} %bitcast.35), calls=%async_computation.1 | async-start | bytes 8388608 | tf_op jit(solution)/shard_map/all_to_all | solution.py:47
  232.8 0.0 copy-done
  232.8 0.8 gather_fusion
  233.6 0.0 copy-done.2
  233.6 0.6 dynamic-slice.2
  234.2 0.6 broadcast_add_fusion
  234.8 0.1 broadcast_subtract_fusion
  234.8 94.8 %all-to-all-done.1 = f32[1,8,64,2048]{3,2,0,1:T(8,128)} async-done(((f32[1,8,64,2048]{3,2,0,1:T(8,128)}), f32[1,8,64,2048]{3,2,0,1:T(8,128)}, u32[]{:S(2)}, u32[]{:S(2)}) %all-to-all-start.1) | async-done | bytes 4194336 | tf_op jit(solution)/shard_map/all_to_all | solution.py:47
  329.6 6.1 %divide_bitcast_fusion = f32[1,8,64,2048]{3,2,1,0:T(8,128)} fusion(f32[1,8,64,2048]{3,2,0,1:T(8,128)} %all-to-all-done.1, f32[2048]{0:T(1024)S(1)} %copy-done, f32[8,64]{1,0:T(8,128)S(1)} %broadcast_subtract_fusion, f32[1,8,64,2048]{3,2,1,0:T(8,128)} %reshape.79), kind=kLoop, calls=%fused_computation.5 | loop fusion | flops 3145728 | bytes 12593152 | tf_op jit(solution)/shard_map/div | solution.py:48
  (2 shorter events, 0.0 us)
Async XLA Ops:
  6.5 65.0 %all-gather.3.cloned.1.call-start = ((), (), s32[]{:S(2)}) async-start(), calls=%async_computation.2 | async-start | bytes 4718592 | tf_op jit(solution)/shard_map/all_gather | solution.py:31
  7.3 143.7 %all-gather.5.cloned.1.call-start = ((), (), s32[]{:S(2)}) async-start(), calls=%async_computation.3 | async-start | bytes 17301504 | tf_op jit(solution)/shard_map/all_gather | solution.py:34
  150.9 57.1 %copy-start.1 = (s32[32]{0:T(128)S(1)}, s32[32]{0:T(128)}, u32[]{:S(2)}) copy-start(s32[32]{0:T(128)} %param.7) | copy-start | bytes 388
  225.9 6.9 %copy-start = (f32[2048]{0:T(1024)S(1)}, f32[2048]{0:T(1024)}, u32[]{:S(2)}) copy-start(f32[2048]{0:T(1024)} %param.9) | copy-start | bytes 24580
  225.9 7.7 %copy-start.2 = (f32[8]{0:T(128)S(1)}, f32[8]{0:T(128)}, u32[]{:S(2)}) copy-start(f32[8]{0:T(128)} %param.8) | copy-start | bytes 100
  225.9 103.7 %all-to-all-start.1 = ((f32[1,8,64,2048]{3,2,0,1:T(8,128)}), f32[1,8,64,2048]{3,2,0,1:T(8,128)}, u32[]{:S(2)}, u32[]{:S(2)}) async-start(f32[1,8,64,2048]{3,2,0,1:T(8,128)} %bitcast.35), calls=%async_computation.1 | async-start | bytes 8388608 | tf_op jit(solution)/shard_map/all_to_all | solution.py:47
Sparse Core Ops, SparseCore 0:
  9.1 62.3 all-gather.2
  74.1 76.7 all-gather.4
where the time goes:
time: 343 us
  waiting for transfers between devices  212 us (62%)
  matrix products  67.2 us (20%)
  blocking collectives  26.2 us (8%)
  between operations  13.4 us (4%)
  local copies, waits for them, and re-layouts  10 us (3%)
  starting transfers between devices  6.91 us (2%)
  other arithmetic  6.76 us (2%)
    all_to_all x1, waiting for transfers between devices, body(): lax.all_to_all(direct, 'virt', split_axis=1, concat_axis=1, tiled=True)  94.8 us
    all_gather x1, waiting for transfers between devices, body(): lax.all_gather(own_rows, 'pair', axis=1, tiled=True)  79.3 us
    dot_general x1, matrix products, body(): jnp.einsum('xac,jbc->xjba', lax.all_gather(own_rows, 'pair', axis=1, tile...  57.1 us
    all_gather x1, waiting for transfers between devices, body(): int_full = lax.all_gather(ints, 'virt', axis=2, tiled=True)  37.2 us
    all_to_all x1, blocking collectives, body(): lax.all_to_all(amps, 'virt', split_axis=0, concat_axis=2, tiled=True)  26.2 us
    dot_general x1, matrix products, body(): jnp.einsum('xjbqp,qn->xjbnp', grouped, placing, precision=lax.Precision.H...  10.1 us
    reshape x1, local copies, waits for them, and re-layouts, body(): direct = jnp.einsum('xjbqp,qn->xjbnp', grouped, placing, precision=lax.Pr...  7.81 us
    all_to_all x1, starting transfers between devices, body(): lax.all_to_all(direct, 'virt', split_axis=1, concat_axis=1, tiled=True)  6.87 us
  transfers between devices with their start and end apart: 3, of which 3 were waited for; matrix products, arithmetic and copies ran while one was open for 1% of the time, Pallas kernels for 0%

commit v1 on v0

v1 whole, which is shorter than its diff:
```python
import functools

import jax
import jax.numpy as jnp
from jax import lax
from jax.experimental import pallas as pl
from jax.experimental.pallas import tpu as pltpu
from jax.sharding import PartitionSpec as P

CHUNKS = 4
RING = 8
NT = (((1,), (1,)), ((), ()))
SMEM = pl.BlockSpec(memory_space=pltpu.SMEM)
HBM = pl.BlockSpec(memory_space=pltpu.HBM)
VMEM = pl.BlockSpec(memory_space=pltpu.VMEM)


def split(x):
    high = x.astype(jnp.bfloat16)
    return high, (x - high.astype(jnp.float32)).astype(jnp.bfloat16)


def product_kernel(dims, pos, panel_of, amp_hbm, *refs):
    count, rows, occ, panel, width = dims
    ints = refs[: 2 * RING]
    out_hbm, amp, a_hi, a_lo, i_hi, i_lo, total, packed, sem, out_sem = refs[2 * RING :]
    v = pos[0]
    half = occ // 2

    def start(q, carry):
        pltpu.make_async_copy(amp_hbm.at[q], amp.at[panel_of[q]], sem).start()
        return carry

    lax.fori_loop(0, count, start, 0)
    for s in range(RING):
        for part in range(2):
            block = ints[2 * s + part]
            hi, lo = split(block[...].reshape(half * panel, width))
            at = slice(part * half * panel, (part + 1) * half * panel)
            i_hi[at, s * width : (s + 1) * width] = hi
            i_lo[at, s * width : (s + 1) * width] = lo
    pltpu.make_async_copy(amp_hbm, amp, sem).wait()
    for s in range(RING):
        source = lax.rem(v - s + RING, RING)
        hi, lo = split(amp[:, source].reshape(count * rows, width))
        a_hi[:, s * width : (s + 1) * width] = hi
        a_lo[:, s * width : (s + 1) * width] = lo
    dot = functools.partial(lax.dot_general, dimension_numbers=NT, preferred_element_type=jnp.float32)
    step = count * rows // 2
    for m in range(2):
        at = slice(m * step, (m + 1) * step)
        total[at] = dot(a_hi[at], i_lo[...]) + dot(a_lo[at], i_hi[...]) + dot(a_hi[at], i_hi[...])
    lane = lax.broadcasted_iota(jnp.int32, (step, 2 * panel), 1)
    for p in range(occ // 2):
        cols = slice(2 * panel * p, 2 * panel * (p + 1))
        top, low = total[:step, cols], total[step:, cols]
        packed[2 * p] = jnp.where(lane < panel, top, pltpu.roll(low, panel, 1))
        packed[2 * p + 1] = jnp.where(lane < panel, pltpu.roll(top, panel, 1), low)
    copy = pltpu.make_async_copy(packed, out_hbm, out_sem)
    copy.start()
    copy.wait()


def finish_kernel(dims, pos, e_occ, e_b, e_vir, *refs):
    rows, occ, panel, virtuals = dims
    direct, mirror = refs[:CHUNKS], refs[CHUNKS : 2 * CHUNKS]
    out_hbm, dir_v, mir_v, out_v, in_sem, out_sem = refs[2 * CHUNKS :]
    v = pos[0]
    loads = [
        [pltpu.make_async_copy(direct[k].at[j], dir_v.at[j, k], in_sem.at[j, k]) for k in range(CHUNKS)]
        + [pltpu.make_async_copy(mirror[k].at[j], mir_v.at[j, k], in_sem.at[j, CHUNKS + k]) for k in range(CHUNKS)]
        for j in range(occ)
    ]
    for j in range(occ):
        for copy in loads[j]:
            copy.start()
    lanes = 2 * panel
    for j in range(occ):
        for copy in loads[j]:
            copy.wait()
        base = (e_occ[v] + e_occ[j]) - e_b[...]
        for t in range(virtuals // 2 // lanes):
            parts = []
            for m in (2 * t, 2 * t + 1):
                for k in range(CHUNKS):
                    at = slice(m * rows, (m + 1) * rows)
                    parts.append(dir_v[j, k, at, :] - mir_v[j, k, at, :])
            block = jnp.concatenate(parts, axis=0).T
            for h in range(2):
                cols = slice(h * virtuals // 2 + t * lanes, h * virtuals // 2 + (t + 1) * lanes)
                out_v[j, :, cols] = block[h * panel : (h + 1) * panel, :] / (base - e_vir[:, cols])
        pltpu.make_async_copy(out_v.at[j], out_hbm.at[j], out_sem.at[j]).start()
    for j in range(occ):
        pltpu.make_async_copy(out_v.at[j], out_hbm.at[j], out_sem.at[j]).wait()


def body(amps, ints, panel_of, e_occ, e_vir):
    occ, panel, width = amps.shape
    virtuals = e_vir.shape[0]
    count = panel_of.shape[0]
    rows = panel // CHUNKS
    pos = lax.axis_index("virt").astype(jnp.int32).reshape(1)
    half = occ // 2

    def shift(x, d):
        return lax.ppermute(x, "virt", [(i, (i + d) % RING) for i in range(RING)])

    pieces = {}
    for part in range(2):
        mine = ints[part * half : (part + 1) * half]
        pieces[0, part] = mine
        up = down = mine
        for s in range(1, RING // 2 + 1):
            if s < RING // 2 or part == 0:
                up = shift(up, 1)
                pieces[s, part] = up
            if s < RING // 2 or part == 1:
                down = shift(down, -1)
                pieces[RING - s, part] = down
    held = [pieces[s, part] for s in range(RING) for part in range(2)]

    own = lax.all_to_all(amps, "virt", split_axis=0, concat_axis=0, tiled=True)
    own, *_ = lax.optimization_barrier([own] + [pieces[s, part] for s in (1, RING - 1) for part in range(2)])
    f32, bf16 = jnp.float32, jnp.bfloat16
    packed = jax.ShapeDtypeStruct((occ, count * rows // 2, 2 * panel), f32)
    direct, mirror = [], []
    for k in range(CHUNKS):
        amp_all = lax.all_gather(own[:, k * rows : (k + 1) * rows, :], "pair", axis=0)
        out = pl.pallas_call(
            functools.partial(product_kernel, (count, rows, occ, panel, width)),
            out_shape=packed,
            in_specs=[SMEM, SMEM, HBM] + [VMEM] * (2 * RING),
            out_specs=HBM,
            scratch_shapes=[
                pltpu.VMEM((count, RING, rows, width), f32),
                pltpu.VMEM((count * rows, RING * width), bf16),
                pltpu.VMEM((count * rows, RING * width), bf16),
                pltpu.VMEM((occ * panel, RING * width), bf16),
                pltpu.VMEM((occ * panel, RING * width), bf16),
                pltpu.VMEM((count * rows, occ * panel), f32),
                pltpu.VMEM(packed.shape, f32),
                pltpu.SemaphoreType.DMA,
                pltpu.SemaphoreType.DMA,
            ],
            compiler_params=pltpu.CompilerParams(vmem_limit_bytes=48 * 2**20),
            name=f"product_{k}",
        )(pos, panel_of, amp_all, *held)
        direct.append(out)
        mirror.append(lax.all_to_all(out, "virt", split_axis=0, concat_axis=0, tiled=True))

    e_b = lax.dynamic_slice(e_vir, (lax.axis_index("pair") * panel,), (panel,)).reshape(panel, 1)
    out = pl.pallas_call(
        functools.partial(finish_kernel, (rows, occ, panel, virtuals)),
        out_shape=jax.ShapeDtypeStruct((occ, panel, virtuals), f32),
        in_specs=[SMEM, SMEM, VMEM, VMEM] + [HBM] * (2 * CHUNKS),
        out_specs=HBM,
        scratch_shapes=[
            pltpu.VMEM((occ, CHUNKS) + packed.shape[1:], f32),
            pltpu.VMEM((occ, CHUNKS) + packed.shape[1:], f32),
            pltpu.VMEM((occ, panel, virtuals), f32),
            pltpu.SemaphoreType.DMA((occ, 2 * CHUNKS)),
            pltpu.SemaphoreType.DMA((occ,)),
        ],
        compiler_params=pltpu.CompilerParams(vmem_limit_bytes=48 * 2**20),
        name="finish",
    )(pos, e_occ, e_b, e_vir.reshape(1, virtuals), *direct, *mirror)
    return out[None]


def solution(mesh):
    in_specs = (P(None, "pair", "virt"), P(None, "pair", "virt"), P(), P(), P())
    out_specs = P("virt", None, "pair", None)
    return jax.shard_map(body, mesh=mesh, in_specs=in_specs, out_specs=out_specs, check_vma=False)
```

time: 343 us -> 311 us (0.907)
  matrix products: 67.2 us -> 0 us
  starting transfers between devices: 6.91 us -> 53.9 us
  Pallas kernels: 0 us -> 38.5 us
  blocking collectives: 26.2 us -> 0 us
  waiting for transfers between devices: 212 us -> 201 us
  other arithmetic: 6.76 us -> 0 us
  local copies, waits for them, and re-layouts: 10 us -> 3.69 us
    dot_general x2 -> x0, matrix products: 67.2 us -> none  [the longest x1 57.1 us: body(): jnp.einsum('xac,jbc->xjba', lax.all_gather(own_rows, 'pair', axis=1, tile...]
    all_to_all x1 -> x5, waiting for transfers between devices: 94.8 us -> 29.1 us  [the longest x4 29.1 us: body(): lax.all_to_all(out, 'virt', split_axis=0, concat_axis=0, tiled=True)]
    pallas_call x0 -> x5, Pallas kernels: none -> 38.5 us  [the longest x4 31.9 us: body(): pl.pallas_call(functools.partial(product_kernel, (count, rows, occ, panel...]
    ppermute x0 -> x14, waiting for transfers between devices: none -> 36.9 us  [shift(): return lax.ppermute(x, 'virt', [(i, (i + d) % RING) for i in range(RING)])]
    all_to_all x1 -> x5, starting transfers between devices: 6.87 us -> 36 us  [the longest x4 27 us: body(): lax.all_to_all(out, 'virt', split_axis=0, concat_axis=0, tiled=True)]
    all_to_all x1 -> x0, blocking collectives: 26.2 us -> none  [body(): lax.all_to_all(amps, 'virt', split_axis=0, concat_axis=2, tiled=True)]
    ppermute x0 -> x14, starting transfers between devices: none -> 17.7 us  [shift(): return lax.ppermute(x, 'virt', [(i, (i + d) % RING) for i in range(RING)])]
    all_gather x2 -> x4, waiting for transfers between devices: 117 us -> 133 us  [body(): amp_all = lax.all_gather(own[:, k * rows:(k + 1) * rows, :], 'pair', axis=0)]
  transfers between devices with their start and end apart: 3 -> 23, of which waited for: 3 -> 12; matrix products, arithmetic and copies ran while one was open for 1% -> 0% of each run, Pallas kernels for 0% -> 10%
where the time goes in v1:
time: 311 us
  waiting for transfers between devices  201 us (65%)
  starting transfers between devices  53.9 us (17%)
  Pallas kernels  38.5 us (12%)
  between operations  13.2 us (4%)
  local copies, waits for them, and re-layouts  3.69 us (1%)
    all_gather x4, waiting for transfers between devices, body(): amp_all = lax.all_gather(own[:, k * rows:(k + 1) * rows, :], 'pair', axis=0)  133 us
    ppermute x14, waiting for transfers between devices, shift(): return lax.ppermute(x, 'virt', [(i, (i + d) % RING) for i in range(RING)])  36.9 us
    pallas_call x4, Pallas kernels, body(): pl.pallas_call(functools.partial(product_kernel, (count, rows, occ, panel...  31.9 us
    all_to_all x4, waiting for transfers between devices, body(): lax.all_to_all(out, 'virt', split_axis=0, concat_axis=0, tiled=True)  29.1 us
    all_to_all x4, starting transfers between devices, body(): lax.all_to_all(out, 'virt', split_axis=0, concat_axis=0, tiled=True)  27 us
    ppermute x14, starting transfers between devices, shift(): return lax.ppermute(x, 'virt', [(i, (i + d) % RING) for i in range(RING)])  17.7 us
    all_to_all x1, starting transfers between devices, body(): own = lax.all_to_all(amps, 'virt', split_axis=0, concat_axis=0, tiled=True)  9.01 us
    pallas_call x1, Pallas kernels, body(): pl.pallas_call(functools.partial(finish_kernel, (rows, occ, panel, virtua...  6.6 us
  transfers between devices with their start and end apart: 23, of which 12 were waited for; matrix products, arithmetic and copies ran while one was open for 0% of the time, Pallas kernels for 10%

profile of v1, /device:TPU:1, one launch (start us, length us, event | category | flops | bytes accessed | tf_op | source)
XLA Modules:
  0.0 310.7 jit_solution(10341714636262515696)
XLA Ops:
  6.5 9.0 %all-to-all-start = ((f32[8,64,256]{2,1,0:T(8,128)}), f32[8,64,256]{2,1,0:T(8,128)S(1)}, u32[]{:S(2)}, u32[]{:S(2)}) async-start(f32[8,64,256]{2,1,0:T(8,128)} %param.5), calls=%async_computation | async-start | bytes 1048576 | tf_op jit(solution)/shard_map/all_to_all | solution.py:122
  20.9 14.5 %collective-permute-done.refs_2_ = f32[4,64,256]{2,1,0:T(8,128)S(1)} collective-permute-done((f32[4,64,256]{2,1,0:T(8,128)S(1)}, f32[4,64,256]{2,1,0:T(8,128)S(1)}, u32[]{:S(2)}, u32[]{:S(2)}) %collective-permute-start) | collective-permute-done | bytes 262176 | tf_op jit(solution)/shard_map/ppermute | solution.py:106
  35.5 5.6 %collective-permute-done.1.refs_3_ = f32[4,64,256]{2,1,0:T(8,128)S(1)} collective-permute-done((f32[4,64,256]{2,1,0:T(8,128)S(1)}, f32[4,64,256]{2,1,0:T(8,128)S(1)}, u32[]{:S(2)}, u32[]{:S(2)}) %collective-permute-start.1) | collective-permute-done | bytes 262176 | tf_op jit(solution)/shard_map/ppermute | solution.py:106
  51.6 2.7 collective-permute-start.10
  54.3 2.9 collective-permute-done.5.refs_5_
  57.2 2.7 collective-permute-start.13
  59.9 2.9 collective-permute-done.6.refs_6_
  62.9 2.7 collective-permute-start.11
  65.5 2.9 collective-permute-done.7.refs_7_
  68.5 5.7 %collective-permute-done.8.refs_8_ = f32[4,64,256]{2,1,0:T(8,128)} collective-permute-done((f32[4,64,256]{2,1,0:T(8,128)S(1)}, f32[4,64,256]{2,1,0:T(8,128)}, u32[]{:S(2)}, u32[]{:S(2)}) %collective-permute-start.8) | collective-permute-done | bytes 262176 | tf_op jit(solution)/shard_map/ppermute | solution.py:106
  74.2 19.2 %all-gather.9.cloned.1.call-done = f32[256,16,256]{2,1,0:T(8,128)} async-done(((f32[8,16,256]{2,1,0:T(8,128)}), f32[256,16,256]{2,1,0:T(8,128)}) %all-gather.9.cloned.1.call-update) | async-done | bytes 4194320 | tf_op jit(solution)/shard_map/all_gather | solution.py:128
  94.0 8.0 %product_0.1.refs_0_ = f32[8,256,128]{2,1,0:T(8,128)} custom-call(s32[1]{0:T(128)} %bitcast.pos, s32[32]{0:T(128)S(1)} %copy-done, f32[32,8,16,256]{3,2,1,0:T(8,128)} %bitcast.13, f32[4,64,256]{2,1,0:T(8,128)S(1)} %get-tuple-element.12.refs_0_, f32[4,64,256]{2,1,0:T(8,128)S(1)} %get-tuple-element.11.refs_1_, f32[4,64,256]{2,1,0:T(8,128)S(1)} %collective-permute-done.refs_2_, ...), custom_call_target="tpu_custom_call" | custom-call | tf_op jit(solution)/shard_map/product_0/pallas_call | solution.py:129
  102.0 6.7 %all-to-all-start.1 = ((f32[8,256,128]{2,1,0:T(8,128)}), f32[8,256,128]{2,1,0:T(8,128)}, u32[]{:S(2)}, u32[]{:S(2)}) async-start(f32[8,256,128]{2,1,0:T(8,128)} %product_0.1.refs_0_), calls=%async_computation.1 | async-start | bytes 2097152 | tf_op jit(solution)/shard_map/all_to_all | solution.py:149
  108.8 37.7 %all-gather.11.cloned.1.call-done = f32[256,16,256]{2,1,0:T(8,128)} async-done(((f32[8,16,256]{2,1,0:T(8,128)}), f32[256,16,256]{2,1,0:T(8,128)}) %all-gather.11.cloned.1.call-update) | async-done | bytes 4194320 | tf_op jit(solution)/shard_map/all_gather | solution.py:128
  146.5 8.0 %product_1.1.refs_1_ = f32[8,256,128]{2,1,0:T(8,128)} custom-call(s32[1]{0:T(128)} %bitcast.pos, s32[32]{0:T(128)S(1)} %copy-done.1, f32[32,8,16,256]{3,2,1,0:T(8,128)} %bitcast.12, f32[4,64,256]{2,1,0:T(8,128)S(1)} %get-tuple-element.12.refs_0_, f32[4,64,256]{2,1,0:T(8,128)S(1)} %get-tuple-element.11.refs_1_, ...), custom_call_target="tpu_custom_call" | custom-call | tf_op jit(solution)/shard_map/product_1/pallas_call | solution.py:129
  154.5 6.8 %all-to-all-start.2 = ((f32[8,256,128]{2,1,0:T(8,128)}), f32[8,256,128]{2,1,0:T(8,128)}, u32[]{:S(2)}, u32[]{:S(2)}) async-start(f32[8,256,128]{2,1,0:T(8,128)} %product_1.1.refs_1_), calls=%async_computation.2 | async-start | bytes 2097152 | tf_op jit(solution)/shard_map/all_to_all | solution.py:149
  161.2 38.4 %all-gather.13.cloned.1.call-done = f32[256,16,256]{2,1,0:T(8,128)} async-done(((f32[8,16,256]{2,1,0:T(8,128)}), f32[256,16,256]{2,1,0:T(8,128)}) %all-gather.13.cloned.1.call-update) | async-done | bytes 4194320 | tf_op jit(solution)/shard_map/all_gather | solution.py:128
  199.6 8.0 %product_2.1.refs_2_ = f32[8,256,128]{2,1,0:T(8,128)} custom-call(s32[1]{0:T(128)} %bitcast.pos, s32[32]{0:T(128)S(1)} %copy-done.1, f32[32,8,16,256]{3,2,1,0:T(8,128)} %bitcast.11, f32[4,64,256]{2,1,0:T(8,128)S(1)} %get-tuple-element.12.refs_0_, f32[4,64,256]{2,1,0:T(8,128)S(1)} %get-tuple-element.11.refs_1_, ...), custom_call_target="tpu_custom_call" | custom-call | tf_op jit(solution)/shard_map/product_2/pallas_call | solution.py:129
  207.6 6.7 %all-to-all-start.3 = ((f32[8,256,128]{2,1,0:T(8,128)}), f32[8,256,128]{2,1,0:T(8,128)}, u32[]{:S(2)}, u32[]{:S(2)}) async-start(f32[8,256,128]{2,1,0:T(8,128)} %product_2.1.refs_2_), calls=%async_computation.3 | async-start | bytes 2097152 | tf_op jit(solution)/shard_map/all_to_all | solution.py:149
  214.3 38.2 %all-gather.15.cloned.1.call-done = f32[256,16,256]{2,1,0:T(8,128)} async-done(((f32[8,16,256]{2,1,0:T(8,128)}), f32[256,16,256]{2,1,0:T(8,128)}) %all-gather.15.cloned.1.call-update) | async-done | bytes 4194320 | tf_op jit(solution)/shard_map/all_gather | solution.py:128
  252.6 8.0 %product_3.1.refs_3_ = f32[8,256,128]{2,1,0:T(8,128)} custom-call(s32[1]{0:T(128)} %bitcast.pos, s32[32]{0:T(128)S(1)} %copy-done.1, f32[32,8,16,256]{3,2,1,0:T(8,128)} %bitcast.10, f32[4,64,256]{2,1,0:T(8,128)S(1)} %get-tuple-element.12.refs_0_, f32[4,64,256]{2,1,0:T(8,128)S(1)} %get-tuple-element.11.refs_1_, ...), custom_call_target="tpu_custom_call" | custom-call | tf_op jit(solution)/shard_map/product_3/pallas_call | solution.py:129
  260.6 6.7 %all-to-all-start.4 = ((f32[8,256,128]{2,1,0:T(8,128)}), f32[8,256,128]{2,1,0:T(8,128)S(1)}, u32[]{:S(2)}, u32[]{:S(2)}) async-start(f32[8,256,128]{2,1,0:T(8,128)} %product_3.1.refs_3_), calls=%async_computation.4 | async-start | bytes 2097152 | tf_op jit(solution)/shard_map/all_to_all | solution.py:149
  267.5 29.1 %all-to-all-done.4.refs_7_ = f32[8,256,128]{2,1,0:T(8,128)S(1)} async-done(((f32[8,256,128]{2,1,0:T(8,128)}), f32[8,256,128]{2,1,0:T(8,128)S(1)}, u32[]{:S(2)}, u32[]{:S(2)}) %all-to-all-start.4) | async-done | bytes 1048608 | tf_op jit(solution)/shard_map/all_to_all | solution.py:149
  297.6 6.6 %finish.1 = f32[8,64,2048]{2,1,0:T(8,128)} custom-call(s32[1]{0:T(128)} %bitcast.pos, f32[8]{0:T(128)S(1)} %copy-done.3, f32[64,1]{1,0:T(8,128)S(1)} %copy.7.e_b, f32[1,2048]{1,0:T(1,128)S(1)} %bitcast.9, f32[8,256,128]{2,1,0:T(8,128)} %product_0.1.refs_0_, f32[8,256,128]{2,1,0:T(8,128)} %product_1.1.refs_1_, f32[8,256,128]{2,1,0:T(8,128)} %product_2.1.refs_2_, ...), custom_call_target="tpu_custom_call" | custom-call | tf_op jit(solution)/shard_map/finish/pallas_call | solution.py:152
  (45 shorter events, 17.7 us)
Async XLA Ops:
  6.5 34.6 %all-to-all-start = ((f32[8,64,256]{2,1,0:T(8,128)}), f32[8,64,256]{2,1,0:T(8,128)S(1)}, u32[]{:S(2)}, u32[]{:S(2)}) async-start(f32[8,64,256]{2,1,0:T(8,128)} %param.5), calls=%async_computation | async-start | bytes 1048576 | tf_op jit(solution)/shard_map/all_to_all | solution.py:122
  15.6 77.8 %all-gather.9.cloned.1.call-start = ((), (), s32[]{:S(2)}) async-start(), calls=%async_computation.5 | async-start | bytes 4325376 | tf_op jit(solution)/shard_map/all_gather | solution.py:128
  16.7 18.8 %collective-permute-start = (f32[4,64,256]{2,1,0:T(8,128)S(1)}, f32[4,64,256]{2,1,0:T(8,128)S(1)}, u32[]{:S(2)}, u32[]{:S(2)}) collective-permute-start(f32[4,64,256]{2,1,0:T(8,128)S(1)} %get-tuple-element.12.refs_0_), channel_id=1, source_target_pairs={{0,1},{1,2},{2,3},{3,4},{4,5},{5,6},{6,7},{7,0},{8,9},{9,10},{10,1... | collective-permute-start | bytes 786440 | tf_op jit(solution)/shard_map/ppermute | solution.py:106
  18.2 22.9 %collective-permute-start.1 = (f32[4,64,256]{2,1,0:T(8,128)S(1)}, f32[4,64,256]{2,1,0:T(8,128)S(1)}, u32[]{:S(2)}, u32[]{:S(2)}) collective-permute-start(f32[4,64,256]{2,1,0:T(8,128)S(1)} %get-tuple-element.11.refs_1_), channel_id=1, source_target_pairs={{0,1},{1,2},{2,3},{3,4},{4,5},{5,6},{6,7},{7,0},{8,9},{9,10},{10,1... | collective-permute-start | bytes 786440 | tf_op jit(solution)/shard_map/ppermute | solution.py:106
  19.3 21.8 %collective-permute-start.2 = (f32[4,64,256]{2,1,0:T(8,128)S(1)}, f32[4,64,256]{2,1,0:T(8,128)S(1)}, u32[]{:S(2)}, u32[]{:S(2)}) collective-permute-start(f32[4,64,256]{2,1,0:T(8,128)S(1)} %get-tuple-element.12.refs_0_), channel_id=1, source_target_pairs={{0,7},{1,0},{2,1},{3,2},{4,3},{5,4},{6,5},{7,6},{8,15},{9,8},{10,9... | collective-permute-start | bytes 786440 | tf_op jit(solution)/shard_map/ppermute | solution.py:106
  20.8 20.3 %collective-permute-start.3 = (f32[4,64,256]{2,1,0:T(8,128)S(1)}, f32[4,64,256]{2,1,0:T(8,128)S(1)}, u32[]{:S(2)}, u32[]{:S(2)}) collective-permute-start(f32[4,64,256]{2,1,0:T(8,128)S(1)} %get-tuple-element.11.refs_1_), channel_id=1, source_target_pairs={{0,7},{1,0},{2,1},{3,2},{4,3},{5,4},{6,5},{7,6},{8,15},{9,8},{10,9... | collective-permute-start | bytes 786440 | tf_op jit(solution)/shard_map/ppermute | solution.py:106
  41.9 104.6 %all-gather.11.cloned.1.call-start = ((), (), s32[]{:S(2)}) async-start(), calls=%async_computation.6 | async-start | bytes 4325376 | tf_op jit(solution)/shard_map/all_gather | solution.py:128
  42.7 156.9 %all-gather.13.cloned.1.call-start = ((), (), s32[]{:S(2)}) async-start(), calls=%async_computation.7 | async-start | bytes 4325376 | tf_op jit(solution)/shard_map/all_gather | solution.py:128
  43.4 209.2 %all-gather.15.cloned.1.call-start = ((), (), s32[]{:S(2)}) async-start(), calls=%async_computation.8 | async-start | bytes 4325376 | tf_op jit(solution)/shard_map/all_gather | solution.py:128
  44.0 7.6 %collective-permute-start.4 = (f32[4,64,256]{2,1,0:T(8,128)S(1)}, f32[4,64,256]{2,1,0:T(8,128)S(1)}, u32[]{:S(2)}, u32[]{:S(2)}) collective-permute-start(f32[4,64,256]{2,1,0:T(8,128)S(1)} %collective-permute-done.refs_2_), channel_id=1, source_target_pairs={{0,1},{1,2},{2,3},{3,4},{4,5},{5,6},{6,7},{7,0},{8,9},{9,10},{10,1... | collective-permute-start | bytes 786440 | tf_op jit(solution)/shard_map/ppermute | solution.py:106
  44.1 7.6 %collective-permute-start.9 = (f32[4,64,256]{2,1,0:T(8,128)S(1)}, f32[4,64,256]{2,1,0:T(8,128)S(1)}, u32[]{:S(2)}, u32[]{:S(2)}) collective-permute-start(f32[4,64,256]{2,1,0:T(8,128)S(1)} %collective-permute-done.3.refs_15_), channel_id=1, source_target_pairs={{0,7},{1,0},{2,1},{3,2},{4,3},{5,4},{6,5},{7,6},{8,15},{9,8},{10,9... | collective-permute-start | bytes 786440 | tf_op jit(solution)/shard_map/ppermute | solution.py:106
  46.7 10.5 %collective-permute-start.5 = (f32[4,64,256]{2,1,0:T(8,128)S(1)}, f32[4,64,256]{2,1,0:T(8,128)S(1)}, u32[]{:S(2)}, u32[]{:S(2)}) collective-permute-start(f32[4,64,256]{2,1,0:T(8,128)S(1)} %collective-permute-done.1.refs_3_), channel_id=1, source_target_pairs={{0,1},{1,2},{2,3},{3,4},{4,5},{5,6},{6,7},{7,0},{8,9},{9,10},{10,1... | collective-permute-start | bytes 786440 | tf_op jit(solution)/shard_map/ppermute | solution.py:106
  46.7 10.5 %collective-permute-start.12 = (f32[4,64,256]{2,1,0:T(8,128)S(1)}, f32[4,64,256]{2,1,0:T(8,128)S(1)}, u32[]{:S(2)}, u32[]{:S(2)}) collective-permute-start(f32[4,64,256]{2,1,0:T(8,128)S(1)} %collective-permute-done.2.refs_14_), channel_id=1, source_target_pairs={{0,7},{1,0},{2,1},{3,2},{4,3},{5,4},{6,5},{7,6},{8,15},{9,8},{10,9... | collective-permute-start | bytes 786440 | tf_op jit(solution)/shard_map/ppermute | solution.py:106
  51.6 11.2 %collective-permute-start.6 = (f32[4,64,256]{2,1,0:T(8,128)S(1)}, f32[4,64,256]{2,1,0:T(8,128)S(1)}, u32[]{:S(2)}, u32[]{:S(2)}) collective-permute-start(f32[4,64,256]{2,1,0:T(8,128)S(1)} %collective-permute-done.4.refs_4_), channel_id=1, source_target_pairs={{0,1},{1,2},{2,3},{3,4},{4,5},{5,6},{6,7},{7,0},{8,9},{9,10},{10,1... | collective-permute-start | bytes 786440 | tf_op jit(solution)/shard_map/ppermute | solution.py:106
  51.6 11.2 %collective-permute-start.10 = (f32[4,64,256]{2,1,0:T(8,128)S(1)}, f32[4,64,256]{2,1,0:T(8,128)S(1)}, u32[]{:S(2)}, u32[]{:S(2)}) collective-permute-start(f32[4,64,256]{2,1,0:T(8,128)S(1)} %collective-permute-done.9.refs_13_), channel_id=1, source_target_pairs={{0,7},{1,0},{2,1},{3,2},{4,3},{5,4},{6,5},{7,6},{8,15},{9,8},{10,9... | collective-permute-start | bytes 786440 | tf_op jit(solution)/shard_map/ppermute | solution.py:106
  57.2 11.2 %collective-permute-start.7 = (f32[4,64,256]{2,1,0:T(8,128)S(1)}, f32[4,64,256]{2,1,0:T(8,128)S(1)}, u32[]{:S(2)}, u32[]{:S(2)}) collective-permute-start(f32[4,64,256]{2,1,0:T(8,128)S(1)} %collective-permute-done.5.refs_5_), channel_id=1, source_target_pairs={{0,1},{1,2},{2,3},{3,4},{4,5},{5,6},{6,7},{7,0},{8,9},{9,10},{10,1... | collective-permute-start | bytes 786440 | tf_op jit(solution)/shard_map/ppermute | solution.py:106
  57.2 11.2 %collective-permute-start.13 = (f32[4,64,256]{2,1,0:T(8,128)S(1)}, f32[4,64,256]{2,1,0:T(8,128)}, u32[]{:S(2)}, u32[]{:S(2)}) collective-permute-start(f32[4,64,256]{2,1,0:T(8,128)S(1)} %collective-permute-done.12.refs_12_), channel_id=1, source_target_pairs={{0,7},{1,0},{2,1},{3,2},{4,3},{5,4},{6,5},{7,6},{8,15},{9,8},{10,9... | collective-permute-start | bytes 786440 | tf_op jit(solution)/shard_map/ppermute | solution.py:106
  62.9 11.3 %collective-permute-start.8 = (f32[4,64,256]{2,1,0:T(8,128)S(1)}, f32[4,64,256]{2,1,0:T(8,128)}, u32[]{:S(2)}, u32[]{:S(2)}) collective-permute-start(f32[4,64,256]{2,1,0:T(8,128)S(1)} %collective-permute-done.6.refs_6_), channel_id=1, source_target_pairs={{0,1},{1,2},{2,3},{3,4},{4,5},{5,6},{6,7},{7,0},{8,9},{9,10},{10,1... | collective-permute-start | bytes 786440 | tf_op jit(solution)/shard_map/ppermute | solution.py:106
  62.9 11.3 %collective-permute-start.11 = (f32[4,64,256]{2,1,0:T(8,128)S(1)}, f32[4,64,256]{2,1,0:T(8,128)}, u32[]{:S(2)}, u32[]{:S(2)}) collective-permute-start(f32[4,64,256]{2,1,0:T(8,128)S(1)} %collective-permute-done.10.refs_11_), channel_id=1, source_target_pairs={{0,7},{1,0},{2,1},{3,2},{4,3},{5,4},{6,5},{7,6},{8,15},{9,8},{10,9... | collective-permute-start | bytes 786440 | tf_op jit(solution)/shard_map/ppermute | solution.py:106
  94.0 52.5 %copy-start.1 = (s32[32]{0:T(128)S(1)}, s32[32]{0:T(128)}, u32[]{:S(2)}) copy-start(s32[32]{0:T(128)} %panel_of.7) | copy-start | bytes 388
  102.0 52.4 %all-to-all-start.1 = ((f32[8,256,128]{2,1,0:T(8,128)}), f32[8,256,128]{2,1,0:T(8,128)}, u32[]{:S(2)}, u32[]{:S(2)}) async-start(f32[8,256,128]{2,1,0:T(8,128)} %product_0.1.refs_0_), calls=%async_computation.1 | async-start | bytes 2097152 | tf_op jit(solution)/shard_map/all_to_all | solution.py:149
  154.5 53.1 %all-to-all-start.2 = ((f32[8,256,128]{2,1,0:T(8,128)}), f32[8,256,128]{2,1,0:T(8,128)}, u32[]{:S(2)}, u32[]{:S(2)}) async-start(f32[8,256,128]{2,1,0:T(8,128)} %product_1.1.refs_1_), calls=%async_computation.2 | async-start | bytes 2097152 | tf_op jit(solution)/shard_map/all_to_all | solution.py:149
  207.6 53.0 %all-to-all-start.3 = ((f32[8,256,128]{2,1,0:T(8,128)}), f32[8,256,128]{2,1,0:T(8,128)}, u32[]{:S(2)}, u32[]{:S(2)}) async-start(f32[8,256,128]{2,1,0:T(8,128)} %product_2.1.refs_2_), calls=%async_computation.3 | async-start | bytes 2097152 | tf_op jit(solution)/shard_map/all_to_all | solution.py:149
  260.6 36.0 %all-to-all-start.4 = ((f32[8,256,128]{2,1,0:T(8,128)}), f32[8,256,128]{2,1,0:T(8,128)S(1)}, u32[]{:S(2)}, u32[]{:S(2)}) async-start(f32[8,256,128]{2,1,0:T(8,128)} %product_3.1.refs_3_), calls=%async_computation.4 | async-start | bytes 2097152 | tf_op jit(solution)/shard_map/all_to_all | solution.py:149
  (4 other events, 61.4 us)
Sparse Core Ops, SparseCore 0:
  42.0 51.3 all-gather.8
  95.9 50.5 all-gather.10
  149.0 50.5 all-gather.12
  202.0 50.5 all-gather.14

commit v2 on v0

v2 whole, which is shorter than its diff:
```python
import functools

import jax
import jax.numpy as jnp
from jax import lax
from jax.experimental import pallas as pl
from jax.experimental.pallas import tpu as pltpu
from jax.sharding import PartitionSpec as P

SIDE = 4
CORES = 2
NT = (((1,), (1,)), ((), ()))
SMEM = pl.BlockSpec(memory_space=pltpu.SMEM)
ANY = pl.BlockSpec(memory_space=pl.ANY)
VMEM = pl.BlockSpec(memory_space=pltpu.VMEM)
LIMIT = pltpu.CompilerParams(vmem_limit_bytes=48 * 2**20)
ROUTES = [
    [((1, 0), (1, 0)), ((-1, 0), (-1, 0)), ((0, 1), (0, 1)), ((0, -1), (0, -1))],
    [((1, 1), (1, 0)), ((-1, -1), (-1, 0)), ((-1, 1), (0, 1)), ((1, -1), (0, -1)), ((2, 0), (1, 0)), ((0, 2), (0, 1))],
    [((2, 1), (-1, 0)), ((1, 2), (0, -1)), ((2, -1), (1, 0)), ((-1, 2), (0, -1)), ((2, 2), (0, 1))],
]


def wrap(x, y):
    return x % SIDE, y % SIDE


def split(x):
    high = x.astype(jnp.bfloat16)
    return high, (x - high.astype(jnp.float32)).astype(jnp.bfloat16)


def product_kernel(dims, ints_hbm, *refs):
    depth, occ, panel, width, chips = dims
    amps_hbm = refs[:chips]
    out_hbm, ints, amps, i_hi, i_lo, a_hi, a_lo, out, int_sem, amp_sem, out_sem = refs[chips:]
    loads = [pltpu.make_async_copy(amps_hbm[g], amps.at[g], amp_sem.at[g]) for g in range(chips)]
    load = pltpu.make_async_copy(ints_hbm, ints, int_sem)
    load.start()
    for copy in loads:
        copy.start()
    load.wait()
    for s in range(depth):
        cols = slice(s * width, (s + 1) * width)
        i_hi[:, cols], i_lo[:, cols] = split(ints[s].reshape(occ * panel, width))
    for g in range(chips):
        loads[g].wait()
        for e in range(CORES):
            rows = slice((g * CORES + e) * panel, (g * CORES + e + 1) * panel)
            for s in range(depth):
                cols = slice(s * width, (s + 1) * width)
                a_hi[rows, cols], a_lo[rows, cols] = split(amps[g, e, s])
    dot = functools.partial(lax.dot_general, dimension_numbers=NT, preferred_element_type=jnp.float32)
    step = occ * panel // 2
    for m in range(2):
        at = slice(m * step, (m + 1) * step)
        sums = dot(i_hi[at], a_lo[...]) + dot(i_lo[at], a_hi[...]) + dot(i_hi[at], a_hi[...])
        out[m * occ // 2 : (m + 1) * occ // 2] = sums.reshape(occ // 2, panel, chips * CORES * panel)
    copy = pltpu.make_async_copy(out, out_hbm, out_sem)
    copy.start()
    copy.wait()


def finish_kernel(dims, slots, places, panel_of, e_occ, e_b, e_vir, *refs):
    occ, panel, virtuals, widths = dims
    chunks = len(widths)
    direct, mirror = refs[:chunks], refs[chunks : 2 * chunks]
    out_hbm, slot_of, dir_v, mir_v, out_v, in_sem, out_sem = refs[2 * chunks :]
    starts = [sum(widths[:k]) for k in range(chunks)]
    loads = []
    for j in range(occ):
        for k in range(chunks):
            cols = pl.ds(starts[k], widths[k])
            loads.append((j, pltpu.make_async_copy(direct[k].at[j], dir_v.at[j, :, cols], in_sem.at[j, k])))
            loads.append((j, pltpu.make_async_copy(mirror[k].at[j], mir_v.at[j, :, cols], in_sem.at[j, chunks + k])))
    for _, copy in loads:
        copy.start()
    v, x, y, core = places[0], places[1], places[2], places[3]
    for s, ((dx, dy), e) in enumerate(slots):
        chip = lax.rem(x + dx + SIDE, SIDE) * SIDE + lax.rem(y + dy + SIDE, SIDE)
        slot_of[panel_of[chip * CORES + lax.rem(core + e, CORES)]] = s
    lanes = 2 * panel
    lane = lax.broadcasted_iota(jnp.int32, (panel, lanes), 1)
    for j in range(occ):
        for at, copy in loads:
            if at == j:
                copy.wait()
        base = (e_occ[v] + e_occ[j]) - e_b[...]
        for t in range(virtuals // lanes):
            sides = []
            for h in range(2):
                s = slot_of[2 * t + h]
                cols = pl.ds(pl.multiple_of((s // 2) * lanes, lanes), lanes)
                diff = dir_v[j, :, cols] - mir_v[j, :, cols]
                sides.append(pltpu.roll(diff, lax.rem(s + h, 2) * panel, 1))
            cols = slice(t * lanes, (t + 1) * lanes)
            out_v[j, :, cols] = jnp.where(lane < panel, sides[0], sides[1]) / (base - e_vir[:, cols])
        pltpu.make_async_copy(out_v.at[j], out_hbm.at[j], out_sem.at[j]).start()
    for j in range(occ):
        pltpu.make_async_copy(out_v.at[j], out_hbm.at[j], out_sem.at[j]).wait()


def body(amps, ints, panel_of, e_occ, e_vir):
    occ, panel, width = amps.shape
    virtuals = e_vir.shape[0]
    depth = virtuals // width
    f32, bf16 = jnp.float32, jnp.bfloat16
    pair = lax.axis_index("pair").astype(jnp.int32)
    v = lax.axis_index("virt").astype(jnp.int32)
    places = jnp.stack([v, pair // (SIDE * CORES), (pair // CORES) % SIDE, pair % CORES])

    def move(data, dx, dy, dcore=0):
        perm = []
        for x in range(SIDE):
            for y in range(SIDE):
                for c in range(CORES):
                    to = wrap(x + dx, y + dy)
                    perm.append(((x * SIDE + y) * CORES + c, (to[0] * SIDE + to[1]) * CORES + (c + dcore) % CORES))
        return lax.ppermute(data, "pair", perm)

    int_all = lax.all_gather(ints, "virt", axis=0)
    own = lax.all_to_all(amps, "virt", split_axis=0, concat_axis=0, tiled=True)
    held = {(0, 0): jnp.stack([own, move(own, 0, 0, 1)])}
    slots, widths, direct, mirror = [], [], [], []
    for k, routes in enumerate(ROUTES):
        chips = [(0, 0)] if k == 0 else []
        for to, (dx, dy) in routes:
            before = wrap(to[0] - dx, to[1] - dy)
            held[wrap(*to)] = move(held[before], -dx, -dy)
            chips.append(wrap(*to))
        count = len(chips)
        slots += [(chip, e) for chip in chips for e in range(CORES)]
        widths.append(count * CORES * panel)
        shape = (occ, panel, widths[-1])
        out = pl.pallas_call(
            functools.partial(product_kernel, (depth, occ, panel, width, count)),
            out_shape=jax.ShapeDtypeStruct(shape, f32),
            in_specs=[ANY] * (1 + count),
            out_specs=ANY,
            scratch_shapes=[
                pltpu.VMEM((depth, occ, panel, width), f32),
                pltpu.VMEM((count, CORES, depth, panel, width), f32),
                pltpu.VMEM((occ * panel, depth * width), bf16),
                pltpu.VMEM((occ * panel, depth * width), bf16),
                pltpu.VMEM((widths[-1], depth * width), bf16),
                pltpu.VMEM((widths[-1], depth * width), bf16),
                pltpu.VMEM(shape, f32),
                pltpu.SemaphoreType.DMA,
                pltpu.SemaphoreType.DMA((count,)),
                pltpu.SemaphoreType.DMA,
            ],
            compiler_params=LIMIT,
            cost_estimate=pl.CostEstimate(flops=30_000_000_000, transcendentals=0, bytes_accessed=50_000_000),
            name=f"product_{k}",
        )(int_all, *[held[chip] for chip in chips])
        int_all, out, *mirror = lax.optimization_barrier((int_all, out, *mirror))
        direct.append(out)
        mirror.append(lax.all_to_all(out, "virt", split_axis=0, concat_axis=0, tiled=True))

    chunks = len(widths)
    e_b = lax.dynamic_slice(e_vir, (pair * panel,), (panel,)).reshape(panel, 1)
    out = pl.pallas_call(
        functools.partial(finish_kernel, (occ, panel, virtuals, tuple(widths)), slots),
        out_shape=jax.ShapeDtypeStruct((occ, panel, virtuals), f32),
        in_specs=[SMEM, SMEM, SMEM, VMEM, VMEM] + [ANY] * (2 * chunks),
        out_specs=ANY,
        scratch_shapes=[
            pltpu.SMEM((virtuals // panel,), jnp.int32),
            pltpu.VMEM((occ, panel, virtuals), f32),
            pltpu.VMEM((occ, panel, virtuals), f32),
            pltpu.VMEM((occ, panel, virtuals), f32),
            pltpu.SemaphoreType.DMA((occ, 2 * chunks)),
            pltpu.SemaphoreType.DMA((occ,)),
        ],
        compiler_params=LIMIT,
        name="finish",
    )(places, panel_of, e_occ, e_b, e_vir.reshape(1, virtuals), *direct, *mirror)
    return out[None]


def solution(mesh):
    in_specs = (P(None, "pair", "virt"), P(None, "pair", "virt"), P(), P(), P())
    out_specs = P("virt", None, "pair", None)
    return jax.shard_map(body, mesh=mesh, in_specs=in_specs, out_specs=out_specs, check_vma=False)
```

time: 343 us -> 247 us (0.72)
  waiting for transfers between devices: 212 us -> 138 us
  matrix products: 67.2 us -> 0 us
  Pallas kernels: 0 us -> 35 us
  starting transfers between devices: 6.91 us -> 32.2 us
  local copies, waits for them, and re-layouts: 10 us -> 1.51 us
  other arithmetic: 6.76 us -> 0.17 us
    all_gather x2 -> x1, waiting for transfers between devices: 117 us -> 0.01 us  [body(): int_all = lax.all_gather(ints, 'virt', axis=0)]
    ppermute x0 -> x16, waiting for transfers between devices: none -> 79.7 us  [move(): return lax.ppermute(data, 'pair', perm)]
    dot_general x2 -> x0, matrix products: 67.2 us -> none  [the longest x1 57.1 us: body(): jnp.einsum('xac,jbc->xjba', lax.all_gather(own_rows, 'pair', axis=1, tile...]
    all_to_all x1 -> x3, waiting for transfers between devices: 94.8 us -> 57.7 us  [body(): lax.all_to_all(out, 'virt', split_axis=0, concat_axis=0, tiled=True)]
    pallas_call x0 -> x4, Pallas kernels: none -> 35 us  [the longest x3 29.2 us: body(): pl.pallas_call(functools.partial(product_kernel, (depth, occ, panel, widt...]
    ppermute x0 -> x16, starting transfers between devices: none -> 19.9 us  [move(): return lax.ppermute(data, 'pair', perm)]
    reshape x1 -> x2, local copies, waits for them, and re-layouts: 7.81 us -> 0.18 us  [body(): e_b = lax.dynamic_slice(e_vir, (pair * panel,), (panel,)).reshape(panel, 1)]
    div x1 -> x0, other arithmetic: 6.09 us -> none  [body(): return (direct - mirrored) / denom]
  transfers between devices with their start and end apart: 3 -> 20, of which waited for: 3 -> 11; matrix products, arithmetic and copies ran while one was open for 1% -> 0% of each run, Pallas kernels for 0% -> 12%
where the time goes in v2:
time: 247 us
  waiting for transfers between devices  138 us (56%)
  Pallas kernels  35 us (14%)
  starting transfers between devices  32.2 us (13%)
  blocking collectives  26.2 us (11%)
  between operations  13.6 us (6%)
    ppermute x16, waiting for transfers between devices, move(): return lax.ppermute(data, 'pair', perm)  79.7 us
    all_to_all x3, waiting for transfers between devices, body(): lax.all_to_all(out, 'virt', split_axis=0, concat_axis=0, tiled=True)  57.7 us
    pallas_call x3, Pallas kernels, body(): pl.pallas_call(functools.partial(product_kernel, (depth, occ, panel, widt...  29.2 us
    all_to_all x1, blocking collectives, body(): own = lax.all_to_all(amps, 'virt', split_axis=0, concat_axis=0, tiled=True)  26.2 us
    ppermute x16, starting transfers between devices, move(): return lax.ppermute(data, 'pair', perm)  19.9 us
    all_to_all x3, starting transfers between devices, body(): lax.all_to_all(out, 'virt', split_axis=0, concat_axis=0, tiled=True)  12.4 us
    pallas_call x1, Pallas kernels, body(): pl.pallas_call(functools.partial(finish_kernel, (occ, panel, virtuals, tu...  5.89 us
  transfers between devices with their start and end apart: 20, of which 11 were waited for; matrix products, arithmetic and copies ran while one was open for 0% of the time, Pallas kernels for 12%

profile of v2, /device:TPU:1, one launch (start us, length us, event | category | flops | bytes accessed | tf_op | source)
XLA Modules:
  0.0 246.9 jit_solution(1949890023889471249)
XLA Ops:
  7.3 26.2 %all_to_all.20 = f32[8,64,256]{2,1,0:T(8,128)S(1)} all-to-all(f32[8,64,256]{2,1,0:T(8,128)} %param.5), channel_id=1, replica_groups=mesh['pair'=32,'virt'=8] {'virt'}, dimensions={0} | all-to-all | bytes 1048576 | tf_op jit(solution)/shard_map/all_to_all | solution.py:122
  33.4 3.8 %collective-permute-start = (f32[8,64,256]{2,1,0:T(8,128)S(1)}, f32[8,64,256]{2,1,0:T(8,128)S(1)}, u32[]{:S(2)}, u32[]{:S(2)}) collective-permute-start(f32[8,64,256]{2,1,0:T(8,128)S(1)} %all_to_all.20), channel_id=1, source_target_pairs={{0,8},{8,0},{16,24},{24,16},{32,40},{40,32},{48,56},{56,48},{64,72... | collective-permute-start | bytes 1572872 | tf_op jit(solution)/shard_map/ppermute | solution.py:119
  37.3 1.5 collective-permute-done
  38.9 2.6 %collective-permute-start.1 = (f32[2,8,64,256]{3,2,1,0:T(8,128)S(1)}, f32[2,8,64,256]{3,2,1,0:T(8,128)}, u32[]{:S(2)}, u32[]{:S(2)}) collective-permute-start(f32[2,8,64,256]{3,2,1,0:T(8,128)S(1)} %pad_maximum_fusion.refs_0_), channel_id=1, source_target_pairs={{0,192},{8,200},{16,208},{24,216},{32,224},{40,232},{48,240},{56,2... | collective-permute-start | bytes 3145736 | tf_op jit(solution)/shard_map/ppermute | solution.py:119
  41.5 2.9 %collective-permute-start.3 = (f32[2,8,64,256]{3,2,1,0:T(8,128)S(1)}, f32[2,8,64,256]{3,2,1,0:T(8,128)}, u32[]{:S(2)}, u32[]{:S(2)}) collective-permute-start(f32[2,8,64,256]{3,2,1,0:T(8,128)S(1)} %pad_maximum_fusion.refs_0_), channel_id=1, source_target_pairs={{0,48},{8,56},{16,0},{24,8},{32,16},{40,24},{48,32},{56,40},{64,11... | collective-permute-start | bytes 3145736 | tf_op jit(solution)/shard_map/ppermute | solution.py:119
  44.4 19.3 %collective-permute-done.1.refs_1_ = f32[2,8,64,256]{3,2,1,0:T(8,128)} collective-permute-done((f32[2,8,64,256]{3,2,1,0:T(8,128)S(1)}, f32[2,8,64,256]{3,2,1,0:T(8,128)}, u32[]{:S(2)}, u32[]{:S(2)}) %collective-permute-start.1) | collective-permute-done | bytes 1048608 | tf_op jit(solution)/shard_map/ppermute | solution.py:119
  63.7 1.3 collective-permute-start.8
  65.0 1.9 collective-permute-done.2.refs_2_
  66.9 2.9 %collective-permute-start.7 = (f32[2,8,64,256]{3,2,1,0:T(8,128)S(1)}, f32[2,8,64,256]{3,2,1,0:T(8,128)}, u32[]{:S(2)}, u32[]{:S(2)}) collective-permute-start(f32[2,8,64,256]{3,2,1,0:T(8,128)S(1)} %collective-permute-done.2.refs_2_), channel_id=1, source_target_pairs={{0,48},{8,56},{16,0},{24,8},{32,16},{40,24},{48,32},{56,40},{64,11... | collective-permute-start | bytes 3145736 | tf_op jit(solution)/shard_map/ppermute | solution.py:119
  70.2 1.9 collective-permute-start.5
  72.1 19.7 %collective-permute-done.8.refs_3_ = f32[2,8,64,256]{3,2,1,0:T(8,128)S(1)} collective-permute-done((f32[2,8,64,256]{3,2,1,0:T(8,128)}, f32[2,8,64,256]{3,2,1,0:T(8,128)S(1)}, u32[]{:S(2)}, u32[]{:S(2)}) %collective-permute-start.8) | collective-permute-done | bytes 1048608 | tf_op jit(solution)/shard_map/ppermute | solution.py:119
  92.9 9.3 %product_0.1.refs_0_ = f32[8,64,640]{2,1,0:T(8,128)} custom-call(f32[8,8,64,256]{3,2,1,0:T(8,128)} %bitcast.14, f32[2,8,64,256]{3,2,1,0:T(8,128)S(1)} %pad_maximum_fusion.refs_0_, f32[2,8,64,256]{3,2,1,0:T(8,128)} %collective-permute-done.1.refs_1_, f32[2,8,64,256]{3,2,1,0:T(8,128)S(1)} %collective-permute-done.2.refs_2_, ...), custom_call_target="tpu_custom_call" | custom-call | flops 30000001024 | bytes 50000000 | tf_op jit(solution)/shard_map/product_0/pallas_call | solution.py:135
  102.2 3.6 %all-to-all-start.1 = ((f32[8,64,640]{2,1,0:T(8,128)}), f32[8,64,640]{2,1,0:T(8,128)S(1)}, u32[]{:S(2)}, u32[]{:S(2)}) async-start(f32[8,64,640]{2,1,0:T(8,128)} %product_0.1.refs_0_), calls=%async_computation.1 | async-start | bytes 2621440 | tf_op jit(solution)/shard_map/all_to_all | solution.py:158
  105.8 7.5 %collective-permute-done.10.refs_5_ = f32[2,8,64,256]{3,2,1,0:T(8,128)} collective-permute-done((f32[2,8,64,256]{3,2,1,0:T(8,128)}, f32[2,8,64,256]{3,2,1,0:T(8,128)}, u32[]{:S(2)}, u32[]{:S(2)}) %collective-permute-start.10) | collective-permute-done | bytes 1048608 | tf_op jit(solution)/shard_map/ppermute | solution.py:119
  114.0 1.6 collective-permute-start.13
  116.7 21.9 %collective-permute-done.11.refs_0_ = f32[2,8,64,256]{3,2,1,0:T(8,128)} collective-permute-done((f32[2,8,64,256]{3,2,1,0:T(8,128)}, f32[2,8,64,256]{3,2,1,0:T(8,128)}, u32[]{:S(2)}, u32[]{:S(2)}) %collective-permute-start.11) | collective-permute-done | bytes 1048608 | tf_op jit(solution)/shard_map/ppermute | solution.py:119
  138.6 10.2 %product_1.1.refs_1_ = f32[8,64,768]{2,1,0:T(8,128)} custom-call(f32[8,8,64,256]{3,2,1,0:T(8,128)} %bitcast.15, f32[2,8,64,256]{3,2,1,0:T(8,128)} %collective-permute-done.5.refs_0_, f32[2,8,64,256]{3,2,1,0:T(8,128)} %collective-permute-done.6.refs_1_, f32[2,8,64,256]{3,2,1,0:T(8,128)} %collective-permute-done.7.refs_2_, ...), custom_call_target="tpu_custom_call" | custom-call | flops 30000001024 | bytes 50000000 | tf_op jit(solution)/shard_map/product_1/pallas_call | solution.py:135
  148.8 4.5 %all-to-all-start.2 = ((f32[8,64,768]{2,1,0:T(8,128)}), f32[8,64,768]{2,1,0:T(8,128)}, u32[]{:S(2)}, u32[]{:S(2)}) async-start(f32[8,64,768]{2,1,0:T(8,128)} %product_1.1.refs_1_), calls=%async_computation.2 | async-start | bytes 3145728 | tf_op jit(solution)/shard_map/all_to_all | solution.py:158
  153.3 7.1 %collective-permute-done.14.refs_3_ = f32[2,8,64,256]{3,2,1,0:T(8,128)} collective-permute-done((f32[2,8,64,256]{3,2,1,0:T(8,128)}, f32[2,8,64,256]{3,2,1,0:T(8,128)}, u32[]{:S(2)}, u32[]{:S(2)}) %collective-permute-start.14) | collective-permute-done | bytes 1048608 | tf_op jit(solution)/shard_map/ppermute | solution.py:119
  160.8 9.7 %product_2.1.refs_2_ = f32[8,64,640]{2,1,0:T(8,128)} custom-call(f32[8,8,64,256]{3,2,1,0:T(8,128)} %bitcast.16, f32[2,8,64,256]{3,2,1,0:T(8,128)} %collective-permute-done.11.refs_0_, f32[2,8,64,256]{3,2,1,0:T(8,128)S(1)} %collective-permute-done.12.refs_1_, f32[2,8,64,256]{3,2,1,0:T(8,128)} %collective-permute-done.13.refs_2_, ...), custom_call_target="tpu_custom_call" | custom-call | flops 30000001024 | bytes 50000000 | tf_op jit(solution)/shard_map/product_2/pallas_call | solution.py:135
  170.5 23.2 %all-to-all-done.2.refs_4_ = f32[8,64,768]{2,1,0:T(8,128)} async-done(((f32[8,64,768]{2,1,0:T(8,128)}), f32[8,64,768]{2,1,0:T(8,128)}, u32[]{:S(2)}, u32[]{:S(2)}) %all-to-all-start.2) | async-done | bytes 1572896 | tf_op jit(solution)/shard_map/all_to_all | solution.py:158
  193.7 4.3 %all-to-all-start.3 = ((f32[8,64,640]{2,1,0:T(8,128)}), f32[8,64,640]{2,1,0:T(8,128)}, u32[]{:S(2)}, u32[]{:S(2)}) async-start(f32[8,64,640]{2,1,0:T(8,128)} %product_2.1.refs_2_), calls=%async_computation.3 | async-start | bytes 2621440 | tf_op jit(solution)/shard_map/all_to_all | solution.py:158
  198.3 34.5 %all-to-all-done.3.refs_5_ = f32[8,64,640]{2,1,0:T(8,128)} async-done(((f32[8,64,640]{2,1,0:T(8,128)}), f32[8,64,640]{2,1,0:T(8,128)}, u32[]{:S(2)}, u32[]{:S(2)}) %all-to-all-start.3) | async-done | bytes 1310752 | tf_op jit(solution)/shard_map/all_to_all | solution.py:158
  234.1 5.9 %finish.1 = f32[8,64,2048]{2,1,0:T(8,128)} custom-call(s32[4]{0:T(128)S(1)} %pad_add_fusion.places, s32[32]{0:T(128)S(1)} %copy-done.3, f32[8]{0:T(128)S(1)} %copy-done.4, f32[64,1]{1,0:T(8,128)S(1)} %copy.7.e_b, f32[1,2048]{1,0:T(1,128)S(1)} %bitcast.11, f32[8,64,640]{2,1,0:T(8,128)S(1)} %copy-done, f32[8,64,768]{2,1,0:T(8,128)} %product_1.1.refs_1_, ...), custom_call_target="tpu_custom_call" | custom-call | tf_op jit(solution)/shard_map/finish/pallas_call | solution.py:162
  (36 shorter events, 6.0 us)
Async XLA Ops:
  6.5 86.4 %all-gather.3.cloned.1.call-start = ((), (), s32[]{:S(2)}) async-start(), calls=%async_computation.4 | async-start | bytes 4718592 | tf_op jit(solution)/shard_map/all_gather | solution.py:121
  33.4 5.4 %collective-permute-start = (f32[8,64,256]{2,1,0:T(8,128)S(1)}, f32[8,64,256]{2,1,0:T(8,128)S(1)}, u32[]{:S(2)}, u32[]{:S(2)}) collective-permute-start(f32[8,64,256]{2,1,0:T(8,128)S(1)} %all_to_all.20), channel_id=1, source_target_pairs={{0,8},{8,0},{16,24},{24,16},{32,40},{40,32},{48,56},{56,48},{64,72... | collective-permute-start | bytes 1572872 | tf_op jit(solution)/shard_map/ppermute | solution.py:119
  38.9 24.8 %collective-permute-start.1 = (f32[2,8,64,256]{3,2,1,0:T(8,128)S(1)}, f32[2,8,64,256]{3,2,1,0:T(8,128)}, u32[]{:S(2)}, u32[]{:S(2)}) collective-permute-start(f32[2,8,64,256]{3,2,1,0:T(8,128)S(1)} %pad_maximum_fusion.refs_0_), channel_id=1, source_target_pairs={{0,192},{8,200},{16,208},{24,216},{32,224},{40,232},{48,240},{56,2... | collective-permute-start | bytes 3145736 | tf_op jit(solution)/shard_map/ppermute | solution.py:119
  41.5 25.4 %collective-permute-start.2 = (f32[2,8,64,256]{3,2,1,0:T(8,128)S(1)}, f32[2,8,64,256]{3,2,1,0:T(8,128)S(1)}, u32[]{:S(2)}, u32[]{:S(2)}) collective-permute-start(f32[2,8,64,256]{3,2,1,0:T(8,128)S(1)} %pad_maximum_fusion.refs_0_), channel_id=1, source_target_pairs={{0,64},{8,72},{16,80},{24,88},{32,96},{40,104},{48,112},{56,120},{... | collective-permute-start | bytes 3145736 | tf_op jit(solution)/shard_map/ppermute | solution.py:119
  41.5 28.2 %collective-permute-start.3 = (f32[2,8,64,256]{3,2,1,0:T(8,128)S(1)}, f32[2,8,64,256]{3,2,1,0:T(8,128)}, u32[]{:S(2)}, u32[]{:S(2)}) collective-permute-start(f32[2,8,64,256]{3,2,1,0:T(8,128)S(1)} %pad_maximum_fusion.refs_0_), channel_id=1, source_target_pairs={{0,48},{8,56},{16,0},{24,8},{32,16},{40,24},{48,32},{56,40},{64,11... | collective-permute-start | bytes 3145736 | tf_op jit(solution)/shard_map/ppermute | solution.py:119
  44.4 27.7 %collective-permute-start.4 = (f32[2,8,64,256]{3,2,1,0:T(8,128)S(1)}, f32[2,8,64,256]{3,2,1,0:T(8,128)}, u32[]{:S(2)}, u32[]{:S(2)}) collective-permute-start(f32[2,8,64,256]{3,2,1,0:T(8,128)S(1)} %pad_maximum_fusion.refs_0_), channel_id=1, source_target_pairs={{0,16},{8,24},{16,32},{24,40},{32,48},{40,56},{48,0},{56,8},{64,80... | collective-permute-start | bytes 3145736 | tf_op jit(solution)/shard_map/ppermute | solution.py:119
  63.7 28.1 %collective-permute-start.8 = (f32[2,8,64,256]{3,2,1,0:T(8,128)}, f32[2,8,64,256]{3,2,1,0:T(8,128)S(1)}, u32[]{:S(2)}, u32[]{:S(2)}) collective-permute-start(f32[2,8,64,256]{3,2,1,0:T(8,128)} %collective-permute-done.1.refs_1_), channel_id=1, source_target_pairs={{0,16},{8,24},{16,32},{24,40},{32,48},{40,56},{48,0},{56,8},{64,80... | collective-permute-start | bytes 3145736 | tf_op jit(solution)/shard_map/ppermute | solution.py:119
  66.9 24.9 %collective-permute-start.7 = (f32[2,8,64,256]{3,2,1,0:T(8,128)S(1)}, f32[2,8,64,256]{3,2,1,0:T(8,128)}, u32[]{:S(2)}, u32[]{:S(2)}) collective-permute-start(f32[2,8,64,256]{3,2,1,0:T(8,128)S(1)} %collective-permute-done.2.refs_2_), channel_id=1, source_target_pairs={{0,48},{8,56},{16,0},{24,8},{32,16},{40,24},{48,32},{56,40},{64,11... | collective-permute-start | bytes 3145736 | tf_op jit(solution)/shard_map/ppermute | solution.py:119
  69.7 43.6 %collective-permute-start.10 = (f32[2,8,64,256]{3,2,1,0:T(8,128)}, f32[2,8,64,256]{3,2,1,0:T(8,128)}, u32[]{:S(2)}, u32[]{:S(2)}) collective-permute-start(f32[2,8,64,256]{3,2,1,0:T(8,128)} %collective-permute-done.3.refs_3_), channel_id=1, source_target_pairs={{0,48},{8,56},{16,0},{24,8},{32,16},{40,24},{48,32},{56,40},{64,11... | collective-permute-start | bytes 3145736 | tf_op jit(solution)/shard_map/ppermute | solution.py:119
  70.2 43.9 %collective-permute-start.5 = (f32[2,8,64,256]{3,2,1,0:T(8,128)}, f32[2,8,64,256]{3,2,1,0:T(8,128)}, u32[]{:S(2)}, u32[]{:S(2)}) collective-permute-start(f32[2,8,64,256]{3,2,1,0:T(8,128)} %collective-permute-done.3.refs_3_), channel_id=1, source_target_pairs={{0,192},{8,200},{16,208},{24,216},{32,224},{40,232},{48,240},{56,2... | collective-permute-start | bytes 3145736 | tf_op jit(solution)/shard_map/ppermute | solution.py:119
  72.1 66.5 %collective-permute-start.9 = (f32[2,8,64,256]{3,2,1,0:T(8,128)}, f32[2,8,64,256]{3,2,1,0:T(8,128)}, u32[]{:S(2)}, u32[]{:S(2)}) collective-permute-start(f32[2,8,64,256]{3,2,1,0:T(8,128)} %collective-permute-done.1.refs_1_), channel_id=1, source_target_pairs={{0,192},{8,200},{16,208},{24,216},{32,224},{40,232},{48,240},{56,2... | collective-permute-start | bytes 3145736 | tf_op jit(solution)/shard_map/ppermute | solution.py:119
  91.8 24.3 %collective-permute-start.6 = (f32[2,8,64,256]{3,2,1,0:T(8,128)}, f32[2,8,64,256]{3,2,1,0:T(8,128)}, u32[]{:S(2)}, u32[]{:S(2)}) collective-permute-start(f32[2,8,64,256]{3,2,1,0:T(8,128)} %collective-permute-done.4.refs_4_), channel_id=1, source_target_pairs={{0,64},{8,72},{16,80},{24,88},{32,96},{40,104},{48,112},{56,120},{... | collective-permute-start | bytes 3145736 | tf_op jit(solution)/shard_map/ppermute | solution.py:119
  91.8 46.8 %collective-permute-start.11 = (f32[2,8,64,256]{3,2,1,0:T(8,128)}, f32[2,8,64,256]{3,2,1,0:T(8,128)}, u32[]{:S(2)}, u32[]{:S(2)}) collective-permute-start(f32[2,8,64,256]{3,2,1,0:T(8,128)} %collective-permute-done.7.refs_2_), channel_id=1, source_target_pairs={{0,64},{8,72},{16,80},{24,88},{32,96},{40,104},{48,112},{56,120},{... | collective-permute-start | bytes 3145736 | tf_op jit(solution)/shard_map/ppermute | solution.py:119
  102.2 46.6 %all-to-all-start.1 = ((f32[8,64,640]{2,1,0:T(8,128)}), f32[8,64,640]{2,1,0:T(8,128)S(1)}, u32[]{:S(2)}, u32[]{:S(2)}) async-start(f32[8,64,640]{2,1,0:T(8,128)} %product_0.1.refs_0_), calls=%async_computation.1 | async-start | bytes 2621440 | tf_op jit(solution)/shard_map/all_to_all | solution.py:158
  113.3 40.0 %collective-permute-start.12 = (f32[2,8,64,256]{3,2,1,0:T(8,128)S(1)}, f32[2,8,64,256]{3,2,1,0:T(8,128)S(1)}, u32[]{:S(2)}, u32[]{:S(2)}) collective-permute-start(f32[2,8,64,256]{3,2,1,0:T(8,128)S(1)} %collective-permute-done.8.refs_3_), channel_id=1, source_target_pairs={{0,16},{8,24},{16,32},{24,40},{32,48},{40,56},{48,0},{56,8},{64,80... | collective-permute-start | bytes 3145736 | tf_op jit(solution)/shard_map/ppermute | solution.py:119
  114.0 39.3 %collective-permute-start.13 = (f32[2,8,64,256]{3,2,1,0:T(8,128)S(1)}, f32[2,8,64,256]{3,2,1,0:T(8,128)}, u32[]{:S(2)}, u32[]{:S(2)}) collective-permute-start(f32[2,8,64,256]{3,2,1,0:T(8,128)S(1)} %collective-permute-done.8.refs_3_), channel_id=1, source_target_pairs={{0,192},{8,200},{16,208},{24,216},{32,224},{40,232},{48,240},{56,2... | collective-permute-start | bytes 3145736 | tf_op jit(solution)/shard_map/ppermute | solution.py:119
  116.1 44.3 %collective-permute-start.14 = (f32[2,8,64,256]{3,2,1,0:T(8,128)}, f32[2,8,64,256]{3,2,1,0:T(8,128)}, u32[]{:S(2)}, u32[]{:S(2)}) collective-permute-start(f32[2,8,64,256]{3,2,1,0:T(8,128)} %collective-permute-done.6.refs_1_), channel_id=1, source_target_pairs={{0,16},{8,24},{16,32},{24,40},{32,48},{40,56},{48,0},{56,8},{64,80... | collective-permute-start | bytes 3145736 | tf_op jit(solution)/shard_map/ppermute | solution.py:119
  138.6 22.2 %collective-permute-start.15 = (f32[2,8,64,256]{3,2,1,0:T(8,128)}, f32[2,8,64,256]{3,2,1,0:T(8,128)}, u32[]{:S(2)}, u32[]{:S(2)}) collective-permute-start(f32[2,8,64,256]{3,2,1,0:T(8,128)} %collective-permute-done.11.refs_0_), channel_id=1, source_target_pairs={{0,48},{8,56},{16,0},{24,8},{32,16},{40,24},{48,32},{56,40},{64,11... | collective-permute-start | bytes 3145736 | tf_op jit(solution)/shard_map/ppermute | solution.py:119
  148.8 45.0 %all-to-all-start.2 = ((f32[8,64,768]{2,1,0:T(8,128)}), f32[8,64,768]{2,1,0:T(8,128)}, u32[]{:S(2)}, u32[]{:S(2)}) async-start(f32[8,64,768]{2,1,0:T(8,128)} %product_1.1.refs_1_), calls=%async_computation.2 | async-start | bytes 3145728 | tf_op jit(solution)/shard_map/all_to_all | solution.py:158
  170.5 27.6 %copy-start.2 = (f32[2048]{0:T(1024)S(1)}, f32[2048]{0:T(1024)}, u32[]{:S(2)}) copy-start(f32[2048]{0:T(1024)} %param.9) | copy-start | bytes 24580
  170.5 62.3 %copy-start = (f32[8,64,640]{2,1,0:T(8,128)S(1)}, f32[8,64,640]{2,1,0:T(8,128)}, u32[]{:S(2)}) copy-start(f32[8,64,640]{2,1,0:T(8,128)} %product_0.1.refs_0_) | copy-start | bytes 3932164
  170.5 62.3 %copy-start.3 = (s32[32]{0:T(128)S(1)}, s32[32]{0:T(128)}, u32[]{:S(2)}) copy-start(s32[32]{0:T(128)} %panel_of.1) | copy-start | bytes 388
  170.5 62.3 %copy-start.4 = (f32[8]{0:T(128)S(1)}, f32[8]{0:T(128)}, u32[]{:S(2)}) copy-start(f32[8]{0:T(128)} %e_occ.1) | copy-start | bytes 100
  193.7 39.1 %all-to-all-start.3 = ((f32[8,64,640]{2,1,0:T(8,128)}), f32[8,64,640]{2,1,0:T(8,128)}, u32[]{:S(2)}, u32[]{:S(2)}) async-start(f32[8,64,640]{2,1,0:T(8,128)} %product_2.1.refs_2_), calls=%async_computation.3 | async-start | bytes 2621440 | tf_op jit(solution)/shard_map/all_to_all | solution.py:158
  (1 other events, 1.3 us)
Sparse Core Ops, SparseCore 0:
  9.1 62.3 all-gather.2
